TPU v7x, 32 devices: a whole 2x2x4 slice. The times are simulated.
32 devices in a mesh: row: 4 (over x, core), col: 8 (over z, y).
Axes of the slice: x: 2, y: 2, z: 4, core: 2. Of those that a mesh axis runs over, the one named last changes fastest.
Arguments:
- weights: float32 [160, 4, 256, 256], P(('row', 'col')), may hold values from 0.05 to 0.5, as said below
- edges: int32 [160, 4, 256, 256], P(('row', 'col')), may hold values from 0 to 1, as said below
- offsets: int32 [160, 4], P(('row', 'col')), may hold values from 0 to 5, as said below
- counts: int32 [160], P(('row', 'col')), may hold values from 1 to 4, as said below
Outputs:
- support: float32 [160, 4, 256, 256], P(('row', 'col'))
Inputs may be any that keep to these rules, and one draw needn't show every extreme that they name: Slot 0 of every tile row holds 0 (the diagonal tile). The listed slots (below the row's count) hold distinct offsets o with row + o < 160. Slots at or beyond the count hold arbitrary offsets. `counts`: at most 4 and at most the tile columns left in the row; some row has 4. `edges`: in slot 0 every tile is symmetric with a zero diagonal. `weights`: in slot 0 every tile is symmetric.
All inputs are finite; a program needn't handle non-finite values.
Results may differ from a plain program's by a relative error of at most 0.0003.
Values sent between devices are 32-bit elements; how exact they have to be, the bound alone decides.
No kernel may reach another device: no remote copies, remote signals or barrier semaphores. Data moves between devices by JAX's collectives and lax.ppermute only.
A program may use at most 576 MiB of HBM per device.

v0:
```python
import functools

import jax
import jax.numpy as jnp
from jax import lax
from jax.experimental import pallas as pl
from jax.experimental.pallas import tpu as pltpu
from jax.sharding import PartitionSpec as P

BAND = 6
SLAB = BAND - 1
LANES = 128
AXES = ("row", "col")
BACK, FORWARD = 10, 3
MORE = ((0, 0), (2, 1), (8, 6))
BEHIND, AHEAD = 0, 1
JOBS, RAWS, SUMS, DIAGONALS = 0, 1, 2, 3
TARGET, FACTOR, TURNED, PLACE, SUM_SLOT, DIAGONAL = 8, 32, 64, 96, 128, 144
JOB_SLOT, JOB_LEFT, JOB_RIGHT, LIST_SIZE = 160, 272, 384, 512
VMEM_LIMIT = 56 * 1024 * 1024

F32 = jnp.float32
BF16 = jnp.bfloat16
ANY = pl.BlockSpec(memory_space=pl.ANY)
SMEM = pl.BlockSpec(memory_space=pltpu.SMEM)
VMEM = pl.BlockSpec(memory_space=pltpu.VMEM)


def shifted(value, steps):
    count = lax.axis_size(AXES)
    first, last = (max(0, -steps), min(count, count - steps))
    return lax.ppermute(value, AXES, [(source, source + steps) for source in range(first, last)])


def split(value):
    high = value.astype(BF16)
    low = (value - high.astype(F32)).astype(BF16)
    return high, low


def dot(left, right):
    return jnp.dot(left, right, preferred_element_type=F32)


def product(left_high, left_low, right_high, right_low):
    return dot(left_high, right_high) + (dot(left_high, right_low) + dot(left_low, right_high))


def iotas(size):
    rows = lax.broadcasted_iota(jnp.int32, (size, size), 0)
    columns = lax.broadcasted_iota(jnp.int32, (size, size), 1)
    return rows, columns


def folded(tile):
    half = tile.shape[0] // 2
    rows, columns = iotas(half)
    lower_right = tile[half:, half:]
    mixed = jnp.where(rows <= columns, tile[:half, :half], lower_right)
    diagonal = jnp.sum(jnp.where(rows == columns, lower_right, 0.0), axis=0, keepdims=True)
    return mixed, tile[:half, half:], diagonal


def unfold(store, mixed, upper_right, diagonal):
    half = mixed.shape[0]
    rows, columns = iotas(half)
    turned = mixed.T
    store(0, 0, jnp.where(rows <= columns, mixed, turned))
    store(0, half, upper_right)
    store(half, 0, upper_right.T)
    lower_right = jnp.where(rows > columns, mixed, turned)
    store(half, half, jnp.where(rows == columns, diagonal, lower_right))


def slot_table(table, pattern, row, lists):
    for place in range(SLAB * BAND):
        table[place] = -1
    for slot in range(SLAB * lists):
        offset = pattern[row, slot]
        table[jnp.where(offset >= 0, slot // lists * BAND + offset, SLAB * BAND)] = slot


def listing(items, plan, row, first):
    count = jnp.int32(0)
    for i in range(SLAB):
        mask = plan[row, first + i]
        for bit in range(1, BAND):
            items[count] = i * BAND + bit
            count = count + ((mask >> bit) & 1)
    return count


def diagonals_needed(items, first, plan, row):
    count = jnp.int32(0)
    for i in range(SLAB):
        items[first + count] = i
        count = count + (plan[row, i] & 1)
    return count


def slot_copy(source, target, semaphore, slot, lists):
    return pltpu.make_async_copy(source.at[slot // lists, slot % lists], target.at[slot], semaphore)


def call(kernel, **kwargs):
    return pl.pallas_call(
        kernel,
        compiler_params=pltpu.CompilerParams(vmem_limit_bytes=VMEM_LIMIT),
        **kwargs,
    )


def crossing_slot(pattern, row, slot, lists):
    offset = pattern[row, slot]
    return (offset >= 0) & (slot // lists + offset >= SLAB)


def square_kernel(lists, pattern, weights, edges, out, w, e, total, table, sems):
    tile = weights.shape[-1]
    half = tile // 2
    slot_table(table, pattern, 0, lists)

    @pl.loop(0, SLAB * lists)
    def _(slot):
        @pl.when(crossing_slot(pattern, 0, slot, lists))
        def _():
            slot_copy(weights, w, sems.at[0, slot], slot, lists).start()
            slot_copy(edges, e, sems.at[1, slot], slot, lists).start()

    out[SLAB * half :, :] = jnp.zeros((8, tile), F32)
    for j in range(SLAB):
        total[...] = jnp.zeros((tile, tile), F32)

        @pl.loop(j, SLAB)
        def _(i):
            slot = table[i * BAND + SLAB + j - i]

            @pl.when(slot >= 0)
            def _():
                slot_copy(weights, w, sems.at[0, slot], slot, lists).wait()
                slot_copy(edges, e, sems.at[1, slot], slot, lists).wait()
                value = w[slot] * e[slot].astype(F32)
                total[...] += product(*split(value.T), *split(value))

        mixed, upper_right, diagonal = folded(total[...])
        out[j * half : (j + 1) * half, :half] = mixed
        out[j * half : (j + 1) * half, half:] = upper_right
        out[SLAB * half + j : SLAB * half + j + 1, :half] = diagonal


def square_diagonals(pattern, weights, edges):
    _, lists, tile, _ = weights.shape
    return call(
        functools.partial(square_kernel, lists),
        in_specs=[SMEM, ANY, ANY],
        out_specs=VMEM,
        out_shape=jax.ShapeDtypeStruct((SLAB * tile // 2 + 8, tile), F32),
        scratch_shapes=[
            pltpu.VMEM((SLAB * lists, tile, tile), F32),
            pltpu.VMEM((SLAB * lists, tile, tile), jnp.int32),
            pltpu.VMEM((tile, tile), F32),
            pltpu.SMEM((SLAB * BAND + 1,), jnp.int32),
            pltpu.SemaphoreType.DMA((2, SLAB * lists)),
        ],
    )(pattern, weights, edges)


def plan_kernel(lists, patterns, plan, choice):
    offsets = patterns[...]
    slabs = offsets.shape[0]
    lane = lax.broadcasted_iota(jnp.int32, offsets.shape, 1)
    row = lax.broadcasted_iota(jnp.int32, offsets.shape, 0)
    inside = (offsets >= 0) & (lane < SLAB * lists)
    bits = jnp.where(inside, jnp.left_shift(1, jnp.maximum(offsets, 0)), 0)

    def ahead(value, steps):
        return pltpu.roll(value, LANES - steps, 1) if steps else value

    mask = bits
    for a in range(1, lists):
        mask = mask | ahead(bits, a)
    own = [ahead(mask, i * lists) for i in range(SLAB)]
    rows = own + [pltpu.roll(value, slabs - 1, 0) for value in own]

    def has(r, offset):
        return jnp.right_shift(rows[r], offset) & 1

    zero = jnp.zeros_like(mask)
    need = [zero] * SLAB
    for i in range(SLAB):
        for m in range(SLAB - i, BAND):
            middle = i + m
            wanted = zero
            for t in range(BAND):
                target = i + t
                if target >= SLAB:
                    other, offset = (middle, t - m) if m <= t else (target, m - t)
                    used = has(i, t) & has(middle, m) & has(other, offset)
                    wanted = wanted | used
                    place = other - SLAB
                    need[place] = need[place] | jnp.left_shift(used, offset)
                elif m > t:
                    wanted = wanted | (has(i, t) & has(middle, m) & has(target, m - t))
            need[middle - SLAB] = need[middle - SLAB] | jnp.left_shift(wanted, m)
    crossing = [jnp.right_shift(jnp.left_shift(rows[i], i), SLAB) for i in range(SLAB)]
    partial = []
    for j in range(SLAB):
        cover = zero
        for i in range(SLAB):
            cover = cover | jnp.where(jnp.right_shift(crossing[i], j) & 1 == 1, crossing[i], 0)
        listed = jnp.left_shift(rows[SLAB + j], j) & ((1 << SLAB) - (2 << j))
        partial.append(cover & listed)
    def total(group, bits):
        count = zero
        for value in group:
            for bit in bits:
                count = count + (jnp.right_shift(value, bit) & 1)
        return count

    room = jnp.right_shift(2 * BACK - total(need, (0,)), 1)
    extra = []
    for count in (total(need, range(1, BAND)) - room, total(partial, range(1, BAND)) - FORWARD):
        count = jnp.where((lane == 0) & (row < slabs - 1), count, 0)
        extra.append(jnp.max(count.astype(F32)).astype(jnp.int32))
    result = zero
    for place, value in enumerate(need + partial):
        value = pltpu.roll(value, place, 1) if place else value
        result = jnp.where((lane == place) & (row < slabs - 1), value, result)
    plan[...] = result
    level = jnp.int32(0)
    for back, forward in MORE[:-1]:
        level = level + ((extra[0] > back) | (extra[1] > forward)).astype(jnp.int32)
    choice[0] = level


def travel_plan(patterns, lists):
    return call(
        functools.partial(plan_kernel, lists),
        in_specs=[VMEM],
        out_specs=[VMEM, SMEM],
        out_shape=[
            jax.ShapeDtypeStruct(patterns.shape, jnp.int32),
            jax.ShapeDtypeStruct((1,), jnp.int32),
        ],
    )(patterns)


def pack_kernel(
    lists, plan, pattern, weights, edges, message, squares_out, more_tiles_out, more_squares_out,
    w, e, total, halves, table, raw, sums, diagonals, needed, sems, tile_sem, half_sem, total_sem,
):
    tile = weights.shape[-1]
    half = tile // 2
    slots = SLAB * lists
    slot_table(table, pattern, 0, lists)
    raw_count = listing(raw, plan, BEHIND, 0)
    sum_count = listing(sums, plan, AHEAD, SLAB)
    half_count = diagonals_needed(diagonals, 0, plan, BEHIND)
    room = lax.shift_right_logical(2 * BACK - half_count, 1)

    for slot in range(slots + 1):
        needed[slot] = 0

    def factors(k, i):
        first = SLAB + sums[k] // BAND - i
        second = SLAB + sums[k] % BAND - i
        inside = (first < BAND) & (second < BAND)
        left = table[i * BAND + jnp.minimum(first, BAND - 1)]
        right = table[i * BAND + jnp.minimum(second, BAND - 1)]
        return left, right, inside & (left >= 0) & (right >= 0)

    @pl.loop(0, raw_count)
    def _(k):
        needed[table[raw[k]]] = 1

    @pl.loop(0, half_count)
    def _(k):
        needed[table[diagonals[k] * BAND]] = 1

    @pl.loop(0, sum_count)
    def _(k):
        for i in range(SLAB):
            left, right, both = factors(k, i)
            needed[jnp.where(both, left, slots)] = 1
            needed[jnp.where(both, right, slots)] = 1

    @pl.loop(0, slots)
    def _(slot):
        @pl.when(needed[slot] == 1)
        def _():
            slot_copy(weights, w, sems.at[0, slot], slot, lists).start()
            slot_copy(edges, e, sems.at[1, slot], slot, lists).start()

    @pl.loop(0, slots)
    def _(slot):
        @pl.when(needed[slot] == 1)
        def _():
            slot_copy(weights, w, sems.at[0, slot], slot, lists).wait()
            slot_copy(edges, e, sems.at[1, slot], slot, lists).wait()
            w[slot] = w[slot] * e[slot].astype(F32)

    @pl.loop(0, raw_count)
    def _(k):
        source = w.at[table[raw[k]]]

        @pl.when(k < room)
        def _():
            rows = pl.ds(pl.multiple_of(k * tile, tile), tile)
            pltpu.make_async_copy(source, message.at[rows], tile_sem).start()

        @pl.when(k >= room)
        def _():
            rows = pl.ds(pl.multiple_of((k - room) * tile, tile), tile)
            pltpu.make_async_copy(source, more_tiles_out.at[rows], tile_sem).start()

    @pl.loop(0, half_count)
    def _(k):
        mixed, upper_right, _ = folded(w[table[diagonals[k] * BAND]])
        halves[k, :, :half] = mixed
        halves[k, :, half:] = upper_right
        rows = pl.ds(pl.multiple_of((2 * BACK - 1 - k) * half, half), half)
        pltpu.make_async_copy(halves.at[k], message.at[rows], half_sem).start()

    @pl.loop(0, sum_count)
    def _(k):
        total[k] = jnp.zeros((tile, tile), F32)

        @pl.loop(0, SLAB)
        def _(i):
            left, right, both = factors(k, i)

            @pl.when(both)
            def _():
                total[k] += product(*split(w[left].T), *split(w[right]))

        @pl.when(k < FORWARD)
        def _():
            pltpu.make_async_copy(total.at[k], squares_out.at[k], total_sem).start()

        @pl.when(k >= FORWARD)
        def _():
            target = more_squares_out.at[k - FORWARD]
            pltpu.make_async_copy(total.at[k], target, total_sem).start()

    @pl.loop(0, raw_count)
    def _(k):
        pltpu.make_async_copy(w.at[0], message.at[pl.ds(0, tile)], tile_sem).wait()

    @pl.loop(0, half_count)
    def _(k):
        pltpu.make_async_copy(halves.at[0], message.at[pl.ds(0, half)], half_sem).wait()

    @pl.loop(0, sum_count)
    def _(k):
        pltpu.make_async_copy(total.at[k], squares_out.at[0], total_sem).wait()


def pack_tiles(plan, pattern, weights, edges):
    _, lists, tile, _ = weights.shape
    slots = SLAB * lists
    most_back, most_forward = MORE[-1]
    return call(
        functools.partial(pack_kernel, lists),
        in_specs=[SMEM, SMEM, ANY, ANY],
        out_specs=[ANY] * 4,
        out_shape=[
            jax.ShapeDtypeStruct((BACK * tile, tile), F32),
            jax.ShapeDtypeStruct((FORWARD, tile, tile), F32),
            jax.ShapeDtypeStruct((most_back * tile, tile), F32),
            jax.ShapeDtypeStruct((most_forward, tile, tile), F32),
        ],
        scratch_shapes=[
            pltpu.VMEM((slots, tile, tile), F32),
            pltpu.VMEM((slots, tile, tile), jnp.int32),
            pltpu.VMEM((FORWARD + most_forward, tile, tile), F32),
            pltpu.VMEM((SLAB, tile // 2, tile), F32),
            pltpu.SMEM((SLAB * BAND + 1,), jnp.int32),
            pltpu.SMEM((SLAB * BAND,), jnp.int32),
            pltpu.SMEM((SLAB * BAND,), jnp.int32),
            pltpu.SMEM((SLAB + 1,), jnp.int32),
            pltpu.SMEM((slots + 1,), jnp.int32),
            pltpu.SemaphoreType.DMA((2, slots)),
            pltpu.SemaphoreType.DMA,
            pltpu.SemaphoreType.DMA,
            pltpu.SemaphoreType.DMA,
        ],
    )(plan, pattern, weights, edges)


def main_kernel(
    lists, pattern, weights, edges, out, turned_high, turned_low,
    w, e, high, low, total, result, table, sems, out_sem, factor_sem,
):
    tile = weights.shape[-1]
    slots = SLAB * lists
    slot_table(table, pattern, 0, lists)

    @pl.loop(0, slots)
    def _(slot):
        @pl.when(pattern[0, slot] >= 0)
        def _():
            slot_copy(weights, w, sems.at[0, slot], slot, lists).start()
            slot_copy(edges, e, sems.at[1, slot], slot, lists).start()

    def factors(slot):
        return (
            pltpu.make_async_copy(high.at[slot + slots], turned_high.at[slot], factor_sem),
            pltpu.make_async_copy(low.at[slot + slots], turned_low.at[slot], factor_sem),
        )

    @pl.loop(0, slots)
    def _(slot):
        @pl.when(pattern[0, slot] >= 0)
        def _():
            slot_copy(weights, w, sems.at[0, slot], slot, lists).wait()
            slot_copy(edges, e, sems.at[1, slot], slot, lists).wait()
            value = w[slot] * e[slot].astype(F32)
            w[slot] = value
            high[slot], low[slot] = split(value)

            @pl.when(pattern[0, slot] > 0)
            def _():
                high[slot + slots], low[slot + slots] = split(value.T)

            @pl.when(crossing_slot(pattern, 0, slot, lists))
            def _():
                for copy in factors(slot):
                    copy.start()

    def own(row, offset):
        inside = (row >= 0) & (row < SLAB) & (offset >= 0) & (offset < BAND)
        return jnp.where(inside, table[jnp.where(inside, row * BAND + offset, 0)], -1)

    def turned(row, offset):
        slot = own(row, offset)
        return jnp.where(slot >= 0, slot + slots, -1)

    @pl.loop(0, slots)
    def _(slot):
        i = slot // lists
        offset = pattern[0, slot]

        @pl.when(offset >= 0)
        def _():
            total[...] = jnp.zeros((tile, tile), F32)

            @pl.loop(1 - BAND, BAND)
            def _(m):
                left = jnp.where(m < 0, turned(i + m, -m), own(i + m, m))
                right = jnp.where(
                    m <= offset, own(i + m, offset - m), turned(i + offset, m - offset)
                )

                @pl.when((left >= 0) & (right >= 0))
                def _():
                    total[...] += product(high[left], low[left], high[right], low[right])

            result[slot] = w[slot] * total[...]

        @pl.when(offset < 0)
        def _():
            result[slot] = jnp.zeros((tile, tile), F32)

        pltpu.make_async_copy(result.at[slot], out.at[i, slot % lists], out_sem).start()

    @pl.loop(0, slots)
    def _(slot):
        pltpu.make_async_copy(result.at[slot], out.at[slot // lists, slot % lists], out_sem).wait()

        @pl.when(crossing_slot(pattern, 0, slot, lists))
        def _():
            for copy in factors(slot):
                copy.wait()


def main_part(pattern, weights, edges):
    _, lists, tile, _ = weights.shape
    slots = SLAB * lists
    turned = jax.ShapeDtypeStruct((slots, tile, tile), BF16)
    return call(
        functools.partial(main_kernel, lists),
        in_specs=[SMEM, ANY, ANY],
        out_specs=[ANY, ANY, ANY],
        out_shape=[jax.ShapeDtypeStruct(weights.shape, F32), turned, turned],
        scratch_shapes=[
            pltpu.VMEM((slots, tile, tile), F32),
            pltpu.VMEM((slots, tile, tile), jnp.int32),
            pltpu.VMEM((2 * slots, tile, tile), BF16),
            pltpu.VMEM((2 * slots, tile, tile), BF16),
            pltpu.VMEM((tile, tile), F32),
            pltpu.VMEM((slots, tile, tile), F32),
            pltpu.SMEM((SLAB * BAND + 1,), jnp.int32),
            pltpu.SemaphoreType.DMA((2, slots)),
            pltpu.SemaphoreType.DMA,
            pltpu.SemaphoreType.DMA,
        ],
        cost_estimate=pl.CostEstimate(
            flops=6 * 60 * tile**3, bytes_accessed=3 * weights.size * 4, transcendentals=0
        ),
    )(pattern, weights, edges)


def list_kernel(lists, back, forward, again, plan, pattern, out, table, index, raw, sums):
    slots = SLAB * lists
    first_raw = slots + SLAB
    slot_table(table, pattern, 0, lists)
    raw_count = listing(raw, plan, AHEAD, 0)
    sum_count = jnp.minimum(listing(sums, plan, BEHIND, SLAB), forward)
    half_count = diagonals_needed(out, DIAGONAL, plan, AHEAD)
    room = lax.shift_right_logical(2 * BACK - half_count, 1)
    raw_count = jnp.minimum(raw_count, room + (back - BACK))

    for row in range(SLAB):
        index[row * BAND] = slots + row
        for offset in range(1, BAND):
            index[row * BAND + offset] = -1

    @pl.loop(0, raw_count)
    def _(k):
        place = jnp.where(k < room, k, BACK + k - room)
        out[PLACE + k] = place
        index[raw[k]] = first_raw + place

    for place in range(TARGET, PLACE):
        out[place] = 0
    if not again:
        for row in range(SLAB):
            out[TARGET + row * lists] = 1

    def jobs_of(slot, count):
        i = slot // lists
        offset = pattern[0, slot]
        for m in range(1, BAND):
            row = i + m - SLAB
            left = index[jnp.maximum(row, 0) * BAND + m]
            column = i + offset
            straight = m <= offset
            gap = jnp.where(straight, offset - m, m - offset)
            later = straight | (column >= SLAB)
            next_row = jnp.where(straight, row, column - SLAB)
            theirs = index[jnp.clip(next_row, 0, SLAB - 1) * BAND + gap]
            ours = table[jnp.clip(column, 0, SLAB - 1) * BAND + gap]
            right = jnp.where(later, theirs, ours)
            valid = (offset >= 0) & (row >= 0) & (left >= 0) & (right >= 0)
            if again:
                fresh = first_raw + BACK
                valid = valid & ((left >= fresh) | (right >= fresh))
            turned = valid & later & ~straight
            out[JOB_SLOT + count] = slot
            out[JOB_LEFT + count] = left
            out[JOB_RIGHT + count] = jnp.where(turned, right + back, right)
            out[TARGET + jnp.where(valid, slot, slots)] = 1
            out[FACTOR + jnp.where(valid & (right < first_raw), right, first_raw)] = 1
            out[TURNED + jnp.where(turned, right - first_raw, back)] = 1
            count = count + valid.astype(jnp.int32)
        return count

    jobs = lax.fori_loop(0, slots, jobs_of, jnp.int32(0))

    @pl.loop(0, sum_count)
    def _(k):
        slot = table[sums[k] // BAND * BAND + sums[k] % BAND - sums[k] // BAND]
        out[SUM_SLOT + k] = slot
        if again:
            out[TARGET + jnp.where(k >= FORWARD, slot, slots)] = 1
        else:
            out[TARGET + slot] = 1

    out[JOBS] = jobs
    out[RAWS] = raw_count
    out[SUMS] = sum_count
    out[DIAGONALS] = half_count


def product_list(back, forward, again, plan, pattern, lists):
    small = pltpu.SMEM((SLAB * BAND,), jnp.int32)
    return call(
        functools.partial(list_kernel, lists, back, forward, again),
        in_specs=[SMEM, SMEM],
        out_specs=SMEM,
        out_shape=jax.ShapeDtypeStruct((LIST_SIZE,), jnp.int32),
        scratch_shapes=[pltpu.SMEM((SLAB * BAND + 1,), jnp.int32), small, small, small],
    )(plan, pattern)


def rest_kernel(
    lists, again, todo, weights, edges, turned_high, turned_low, squares, message, sums, before, out,
    w, e, high, low, result, sems, out_sem,
):
    tile = weights.shape[-1]
    half = tile // 2
    slots = SLAB * lists
    back = message.shape[0] // tile
    first_raw = slots + SLAB

    def inputs(slot):
        return (
            slot_copy(weights, w, sems.at[0, slot], slot, lists),
            slot_copy(edges, e, sems.at[1, slot], slot, lists),
            slot_copy(before, result, sems.at[2, slot], slot, lists),
        )

    def factors(slot):
        return (
            pltpu.make_async_copy(turned_high.at[slot], high.at[slot], sems.at[3, slot]),
            pltpu.make_async_copy(turned_low.at[slot], low.at[slot], sems.at[4, slot]),
        )

    def output(slot):
        return pltpu.make_async_copy(result.at[slot], out.at[slot // lists, slot % lists], out_sem)

    @pl.loop(0, slots)
    def _(slot):
        @pl.when(todo[FACTOR + slot] == 1)
        def _():
            for copy in factors(slot):
                copy.start()

        @pl.when(todo[TARGET + slot] == 1)
        def _():
            for copy in inputs(slot):
                copy.start()

    @pl.loop(0, todo[DIAGONALS])
    def _(k):
        row = todo[DIAGONAL + k]

        @pl.when(todo[FACTOR + slots + row] == 1)
        def _():
            def store(first, column, quarter):
                part = (slots + row, pl.ds(first, half), pl.ds(column, half))
                high[part], low[part] = split(quarter)

            part = message[pl.ds(pl.multiple_of((2 * BACK - 1 - k) * half, half), half), :]
            unfold(store, part[:, :half], part[:, half:], jnp.zeros((1, half), F32))

    @pl.loop(0, todo[RAWS])
    def _(k):
        place = todo[PLACE + k]
        value = message[pl.ds(pl.multiple_of(place * tile, tile), tile), :]
        high[first_raw + place], low[first_raw + place] = split(value)

        @pl.when(todo[TURNED + place] == 1)
        def _():
            high[first_raw + back + place], low[first_raw + back + place] = split(value.T)

    @pl.loop(0, slots)
    def _(slot):
        @pl.when(todo[FACTOR + slot] == 1)
        def _():
            for copy in factors(slot):
                copy.wait()

        @pl.when(todo[TARGET + slot] == 1)
        def _():
            for copy in inputs(slot):
                copy.wait()
            w[slot] = w[slot] * e[slot].astype(F32)

    @pl.loop(0, 0 if again else SLAB)
    def _(i):
        def store(first, column, quarter):
            part = (i * lists, pl.ds(first, half), pl.ds(column, half))
            result[part] += w[part] * quarter

        part = squares[pl.ds(pl.multiple_of(i * half, half), half), :]
        rows = squares[SLAB * half :, :half]
        row = lax.broadcasted_iota(jnp.int32, rows.shape, 0)
        diagonal = jnp.sum(jnp.where(row == i, rows, 0.0), axis=0, keepdims=True)
        unfold(store, part[:, :half], part[:, half:], diagonal)

    @pl.loop(FORWARD if again else 0, todo[SUMS])
    def _(k):
        slot = todo[SUM_SLOT + k]
        result[slot] += w[slot] * sums[k]

    @pl.loop(0, todo[JOBS])
    def _(job):
        slot, left, right = todo[JOB_SLOT + job], todo[JOB_LEFT + job], todo[JOB_RIGHT + job]
        value = product(high[left], low[left], high[right], low[right])
        result[slot] += w[slot] * value

    @pl.loop(0, slots)
    def _(slot):
        @pl.when(todo[TARGET + slot] == 1)
        def _():
            output(slot).start()

    @pl.loop(0, slots)
    def _(slot):
        @pl.when(todo[TARGET + slot] == 1)
        def _():
            output(slot).wait()


def rest_part(again, todo, weights, edges, high, low, squares, message, sums, before):
    _, lists, tile, _ = weights.shape
    slots = SLAB * lists
    factors = slots + SLAB + 2 * (message.shape[0] // tile)
    return call(
        functools.partial(rest_kernel, lists, again),
        in_specs=[SMEM, ANY, ANY, ANY, ANY, VMEM, VMEM, VMEM, ANY],
        out_specs=ANY,
        out_shape=jax.ShapeDtypeStruct(weights.shape, F32),
        input_output_aliases={8: 0},
        scratch_shapes=[
            pltpu.VMEM((slots, tile, tile), F32),
            pltpu.VMEM((slots, tile, tile), jnp.int32),
            pltpu.VMEM((factors, tile, tile), BF16),
            pltpu.VMEM((factors, tile, tile), BF16),
            pltpu.VMEM((slots, tile, tile), F32),
            pltpu.SemaphoreType.DMA((5, slots)),
            pltpu.SemaphoreType.DMA,
        ],
    )(todo, weights, edges, high, low, squares, message, sums, before)


def merged(value, bits):
    count = lax.axis_size(AXES)
    for bit in bits:
        other = lax.ppermute(value, AXES, [(device, device ^ bit) for device in range(count)])
        value = jnp.maximum(value, other)
    return value


def shards(weights, edges, offsets, counts):
    slab_count, lists = offsets.shape
    tile = weights.shape[-1]
    slabs = lax.axis_size(AXES)
    columns = lax.axis_size(AXES[1])
    bits = [1 << bit for bit in range(slabs.bit_length() - 1)]
    listed = jnp.arange(lists)[None, :] < counts[:, None]
    pattern = jnp.where(listed, offsets, -1).reshape(1, slab_count * lists)
    pattern = jnp.pad(pattern, ((0, 0), (0, LANES - slab_count * lists)), constant_values=-1)
    empty = jnp.full((5, LANES), -1, jnp.int32)
    patterns = jnp.concatenate([shifted(pattern, 1), pattern, shifted(pattern, -1), empty])
    mine = jnp.arange(slabs)[:, None] == lax.axis_index(AXES)
    everyone = merged(jnp.where(mine, pattern, -1), [bit for bit in bits if bit < columns])

    everyone, patterns = lax.optimization_barrier((everyone, patterns))
    plan, _ = travel_plan(patterns, lists)
    message_out, sums_out, more_message, more_sums = pack_tiles(plan, pattern, weights, edges)
    message_out, sums_out, pattern = lax.optimization_barrier((message_out, sums_out, pattern))
    message = shifted(message_out, -1)
    sums = shifted(sums_out, 1)
    squares_out = square_diagonals(pattern, weights, edges)
    squares_out, pattern = lax.optimization_barrier((squares_out, pattern))
    squares = shifted(squares_out, 1)

    todo = product_list(BACK, FORWARD, False, plan, pattern, lists)
    support, high, low = main_part(pattern, weights, edges)
    everyone, support = lax.optimization_barrier((everyone, support))
    _, level = travel_plan(merged(everyone, [bit for bit in bits if bit >= columns]), lists)
    support = rest_part(
        False, todo, weights, edges, high, low, squares, message, sums, support
    )

    def branch(back, forward):
        def run(
            support, plan, pattern, weights, edges, high, low, squares, message, sums, more_message, more_sums
        ):
            if not back:
                return support
            message = jnp.concatenate([message, shifted(more_message[: back * tile], -1)])
            sums = jnp.concatenate([sums, shifted(more_sums[:forward], 1)])
            todo = product_list(BACK + back, FORWARD + forward, True, plan, pattern, lists)
            return rest_part(
                True, todo, weights, edges, high, low, squares, message, sums, support
            )

        return run

    return lax.switch(
        level[0],
        [branch(*sizes) for sizes in MORE],
        support, plan, pattern, weights, edges, high, low, squares, message, sums, more_message, more_sums,
    )


def solution(mesh):
    in_specs = (
        P(AXES, None, None, None),
        P(AXES, None, None, None),
        P(AXES, None),
        P(AXES),
    )
    out_specs = P(AXES, None, None, None)
    return jax.shard_map(shards, mesh=mesh, in_specs=in_specs, out_specs=out_specs, check_vma=False)
```

profile of v0, /device:TPU:13, one launch (start us, length us, event | category | flops | bytes accessed | tf_op | source)
XLA Modules:
  0.0 128.4 jit_solution(11226436864472683792)
XLA Ops:
  0.0 0.7 fusion.1
  0.7 0.1 copy.12
  0.8 0.1 reshape.12
  0.9 0.1 broadcast_select_fusion
  1.0 0.2 collective-permute-start.4
  1.2 2.4 %collective-permute-done.4 = s32[32,128]{1,0:T(8,128)S(1)} collective-permute-done((s32[32,128]{1,0:T(8,128)S(1)}, s32[32,128]{1,0:T(8,128)S(1)}, u32[]{:S(2)}, u32[]{:S(2)}) %collective-permute-start.4) | collective-permute-done | bytes 16416 | tf_op jit(solution)/shard_map/ppermute | solution.py:721
  3.5 0.1 fusion
  3.6 0.2 collective-permute-start.5
  3.8 2.0 %collective-permute-start.8 = (s32[1,128]{1,0:T(1,128)S(1)}, s32[1,128]{1,0:T(1,128)S(1)}, u32[]{:S(2)}, u32[]{:S(2)}) collective-permute-start(s32[1,128]{1,0:T(1,128)S(1)} %get-tuple-element.106.pattern), channel_id=1, source_target_pairs={{1,0},{2,1},{3,2},{4,3},{5,4},{6,5},{7,6},{8,7},{9,8},{10,9},{11,1... | collective-permute-start | bytes 1544 | tf_op jit(solution)/shard_map/ppermute | solution.py:32
  5.8 4.2 %collective-permute-start.7 = (s32[1,128]{1,0:T(1,128)S(1)}, s32[1,128]{1,0:T(1,128)S(1)}, u32[]{:S(2)}, u32[]{:S(2)}) collective-permute-start(s32[1,128]{1,0:T(1,128)S(1)} %get-tuple-element.106.pattern), channel_id=1, source_target_pairs={{0,1},{1,2},{2,3},{3,4},{4,5},{5,6},{6,7},{7,8},{8,9},{9,10},{10,1... | collective-permute-start | bytes 1544 | tf_op jit(solution)/shard_map/ppermute | solution.py:32
  10.0 0.1 pad.16.clone
  10.1 0.1 fusion.3
  10.2 5.3 %collective-permute-start.6 = (s32[32,128]{1,0:T(8,128)S(1)}, s32[32,128]{1,0:T(8,128)S(1)}, u32[]{:S(2)}, u32[]{:S(2)}) collective-permute-start(s32[32,128]{1,0:T(8,128)S(1)} %fusion.3), channel_id=1, source_target_pairs={{0,4},{1,5},{2,6},{3,7},{4,0},{5,1},{6,2},{7,3},{8,12},{9,13},{10,... | collective-permute-start | bytes 49160 | tf_op jit(solution)/shard_map/ppermute | solution.py:721
  15.4 0.0 collective-permute-done.8
  15.4 0.0 collective-permute-done.7
  15.4 0.7 add_add_fusion.patterns
  16.1 0.5 collective-permute-done.6
  16.6 1.6 %shard_map.49 = (s32[8,128]{1,0:T(8,128)S(1)}, s32[1]{0:T(128)}) custom-call(s32[8,128]{1,0:T(8,128)} %add_add_fusion.patterns), custom_call_target="tpu_custom_call" | custom-call | tf_op jit(solution)/shard_map/pallas_call | solution.py:237
  18.1 0.0 slice-start
  18.2 5.0 %shard_map.50 = (f32[2560,256]{1,0:T(8,128)}, f32[3,256,256]{2,1,0:T(8,128)}, f32[2048,256]{1,0:T(8,128)}, f32[6,256,256]{2,1,0:T(8,128)}) custom-call(s32[8,128]{1,0:T(8,128)S(1)} %get-tuple-element.102.plan, s32[1,128]{1,0:T(1,128)S(1)} %get-tuple-element.106.pattern, f32[5,4,256,256]{3,2,1,0:T(8,128)} %weights.7, s32[5,4,256,256]{3,2,1,0:T(8,128)} %edges.7), custom_call_target="tpu_custom_call" | custom-call | tf_op jit(solution)/shard_map/pallas_call | solution.py:362
  23.1 1.9 %collective-permute-start.12 = (f32[2560,256]{1,0:T(8,128)}, f32[2560,256]{1,0:T(8,128)}, u32[]{:S(2)}, u32[]{:S(2)}) collective-permute-start(f32[2560,256]{1,0:T(8,128)} %get-tuple-element.113), channel_id=1, source_target_pairs={{1,0},{2,1},{3,2},{4,3},{5,4},{6,5},{7,6},{8,7},{9,8},{10,9},{11,1... | collective-permute-start | bytes 7864328 | tf_op jit(solution)/shard_map/ppermute | solution.py:32
  25.1 4.3 %collective-permute-start.13 = (f32[3,256,256]{2,1,0:T(8,128)}, f32[3,256,256]{2,1,0:T(8,128)}, u32[]{:S(2)}, u32[]{:S(2)}) collective-permute-start(f32[3,256,256]{2,1,0:T(8,128)} %get-tuple-element.114), channel_id=1, source_target_pairs={{0,1},{1,2},{2,3},{3,4},{4,5},{5,6},{6,7},{7,8},{8,9},{9,10},{10,1... | collective-permute-start | bytes 2359304 | tf_op jit(solution)/shard_map/ppermute | solution.py:32
  29.4 5.7 %shard_map.51 = f32[648,256]{1,0:T(8,128)} custom-call(s32[1,128]{1,0:T(1,128)S(1)} %get-tuple-element.106.pattern, f32[5,4,256,256]{3,2,1,0:T(8,128)S(1)} %bitcast.4, s32[5,4,256,256]{3,2,1,0:T(8,128)} %edges.7), custom_call_target="tpu_custom_call" | custom-call | tf_op jit(solution)/shard_map/pallas_call | solution.py:153
  35.1 3.1 %collective-permute-start.11 = (f32[648,256]{1,0:T(8,128)}, f32[648,256]{1,0:T(8,128)}, u32[]{:S(2)}, u32[]{:S(2)}) collective-permute-start(f32[648,256]{1,0:T(8,128)} %shard_map.51), channel_id=1, source_target_pairs={{0,1},{1,2},{2,3},{3,4},{4,5},{5,6},{6,7},{7,8},{8,9},{9,10},{10,1... | collective-permute-start | bytes 1990664 | tf_op jit(solution)/shard_map/ppermute | solution.py:32
  38.2 26.4 %shard_map.52 = (f32[5,4,256,256]{3,2,1,0:T(8,128)}, bf16[20,256,256]{2,1,0:T(8,128)(2,1)S(1)}, bf16[20,256,256]{2,1,0:T(8,128)(2,1)}) custom-call(s32[1,128]{1,0:T(1,128)S(1)} %get-tuple-element.106.pattern, f32[5,4,256,256]{3,2,1,0:T(8,128)S(1)} %bitcast.4, s32[5,4,256,256]{3,2,1,0:T(8,128)} %edges.7), custom_call_target="tpu_custom_call" | custom-call | flops 6039797760 | bytes 15728640 | tf_op jit(solution)/shard_map/pallas_call | solution.py:480
  64.7 0.1 collective-permute-start.9
  64.7 1.2 collective-permute-done.9
  65.9 3.5 %shard_map.54.todo = s32[512]{0:T(512)} custom-call(s32[8,128]{1,0:T(8,128)S(1)} %get-tuple-element.102.plan, s32[1,128]{1,0:T(1,128)S(1)} %get-tuple-element.106.pattern), custom_call_target="tpu_custom_call" | custom-call | tf_op jit(solution)/shard_map/pallas_call | solution.py:577
  69.4 0.6 max.19.patterns
  70.0 2.0 %shard_map.53 = (s32[32,128]{1,0:T(8,128)}, s32[1]{0:T(128)}) custom-call(s32[32,128]{1,0:T(8,128)} %max.19.patterns), custom_call_target="tpu_custom_call" | custom-call | tf_op jit(solution)/shard_map/pallas_call | solution.py:237
  72.7 43.4 %collective-permute-done.11.squares = f32[648,256]{1,0:T(8,128)} collective-permute-done((f32[648,256]{1,0:T(8,128)}, f32[648,256]{1,0:T(8,128)}, u32[]{:S(2)}, u32[]{:S(2)}) %collective-permute-start.11) | collective-permute-done | bytes 663584 | tf_op jit(solution)/shard_map/ppermute | solution.py:32
  116.1 12.2 %shard_map.55 = f32[5,4,256,256]{3,2,1,0:T(8,128)} custom-call(s32[512]{0:T(512)} %shard_map.54.todo, f32[5,4,256,256]{3,2,1,0:T(8,128)S(1)} %bitcast.4, s32[5,4,256,256]{3,2,1,0:T(8,128)} %edges.7, bf16[20,256,256]{2,1,0:T(8,128)(2,1)S(1)} %get-tuple-element.110.turned_high, ...), custom_call_target="tpu_custom_call", output_to_operand_aliasing={{}: (8, {})} | custom-call | tf_op jit(solution)/shard_map/pallas_call | solution.py:700
  (15 shorter events, 0.1 us)
Async XLA Ops:
  1.0 2.6 %collective-permute-start.4 = (s32[32,128]{1,0:T(8,128)S(1)}, s32[32,128]{1,0:T(8,128)S(1)}, u32[]{:S(2)}, u32[]{:S(2)}) collective-permute-start(s32[32,128]{1,0:T(8,128)S(1)} %broadcast_select_fusion), channel_id=1, source_target_pairs={{0,1},{1,0},{2,3},{3,2},{4,5},{5,4},{6,7},{7,6},{8,9},{9,8},{10,11... | collective-permute-start | bytes 49160 | tf_op jit(solution)/shard_map/ppermute | solution.py:721
  3.6 6.5 %collective-permute-start.5 = (s32[32,128]{1,0:T(8,128)S(1)}, s32[32,128]{1,0:T(8,128)S(1)}, u32[]{:S(2)}, u32[]{:S(2)}) collective-permute-start(s32[32,128]{1,0:T(8,128)S(1)} %fusion), channel_id=1, source_target_pairs={{0,2},{1,3},{2,0},{3,1},{4,6},{5,7},{6,4},{7,5},{8,10},{9,11},{10,... | collective-permute-start | bytes 49160 | tf_op jit(solution)/shard_map/ppermute | solution.py:721
  3.8 11.6 %collective-permute-start.8 = (s32[1,128]{1,0:T(1,128)S(1)}, s32[1,128]{1,0:T(1,128)S(1)}, u32[]{:S(2)}, u32[]{:S(2)}) collective-permute-start(s32[1,128]{1,0:T(1,128)S(1)} %get-tuple-element.106.pattern), channel_id=1, source_target_pairs={{1,0},{2,1},{3,2},{4,3},{5,4},{6,5},{7,6},{8,7},{9,8},{10,9},{11,1... | collective-permute-start | bytes 1544 | tf_op jit(solution)/shard_map/ppermute | solution.py:32
  5.8 9.7 %collective-permute-start.7 = (s32[1,128]{1,0:T(1,128)S(1)}, s32[1,128]{1,0:T(1,128)S(1)}, u32[]{:S(2)}, u32[]{:S(2)}) collective-permute-start(s32[1,128]{1,0:T(1,128)S(1)} %get-tuple-element.106.pattern), channel_id=1, source_target_pairs={{0,1},{1,2},{2,3},{3,4},{4,5},{5,6},{6,7},{7,8},{8,9},{9,10},{10,1... | collective-permute-start | bytes 1544 | tf_op jit(solution)/shard_map/ppermute | solution.py:32
  10.2 6.4 %collective-permute-start.6 = (s32[32,128]{1,0:T(8,128)S(1)}, s32[32,128]{1,0:T(8,128)S(1)}, u32[]{:S(2)}, u32[]{:S(2)}) collective-permute-start(s32[32,128]{1,0:T(8,128)S(1)} %fusion.3), channel_id=1, source_target_pairs={{0,4},{1,5},{2,6},{3,7},{4,0},{5,1},{6,2},{7,3},{8,12},{9,13},{10,... | collective-permute-start | bytes 49160 | tf_op jit(solution)/shard_map/ppermute | solution.py:721
  18.1 11.2 %slice-start = ((s8[5242880]{0:T(1024)(128)(4,1)}), s8[4194304]{0:T(1024)(128)(4,1)S(1)}, s32[]{:S(2)}) async-start(s8[5242880]{0:T(1024)(128)(4,1)} %bitcast.3), calls=%async_computation | async-start | bytes 8388608
  18.2 11.2 %slice-start.1 = ((s8[5242880]{0:T(1024)(128)(4,1)}), s8[1048576]{0:T(1024)(128)(4,1)S(1)}, s32[]{:S(2)}) async-start(s8[5242880]{0:T(1024)(128)(4,1)} %bitcast.3), calls=%async_computation.1 | async-start | bytes 2097152
  23.1 93.0 %collective-permute-start.12 = (f32[2560,256]{1,0:T(8,128)}, f32[2560,256]{1,0:T(8,128)}, u32[]{:S(2)}, u32[]{:S(2)}) collective-permute-start(f32[2560,256]{1,0:T(8,128)} %get-tuple-element.113), channel_id=1, source_target_pairs={{1,0},{2,1},{3,2},{4,3},{5,4},{6,5},{7,6},{8,7},{9,8},{10,9},{11,1... | collective-permute-start | bytes 7864328 | tf_op jit(solution)/shard_map/ppermute | solution.py:32
  25.1 91.0 %collective-permute-start.13 = (f32[3,256,256]{2,1,0:T(8,128)}, f32[3,256,256]{2,1,0:T(8,128)}, u32[]{:S(2)}, u32[]{:S(2)}) collective-permute-start(f32[3,256,256]{2,1,0:T(8,128)} %get-tuple-element.114), channel_id=1, source_target_pairs={{0,1},{1,2},{2,3},{3,4},{4,5},{5,6},{6,7},{7,8},{8,9},{9,10},{10,1... | collective-permute-start | bytes 2359304 | tf_op jit(solution)/shard_map/ppermute | solution.py:32
  35.1 81.0 %collective-permute-start.11 = (f32[648,256]{1,0:T(8,128)}, f32[648,256]{1,0:T(8,128)}, u32[]{:S(2)}, u32[]{:S(2)}) collective-permute-start(f32[648,256]{1,0:T(8,128)} %shard_map.51), channel_id=1, source_target_pairs={{0,1},{1,2},{2,3},{3,4},{4,5},{5,6},{6,7},{7,8},{8,9},{9,10},{10,1... | collective-permute-start | bytes 1990664 | tf_op jit(solution)/shard_map/ppermute | solution.py:32
  64.7 1.2 collective-permute-start.9
  65.9 3.5 %collective-permute-start.10 = (s32[32,128]{1,0:T(8,128)S(1)}, s32[32,128]{1,0:T(8,128)S(1)}, u32[]{:S(2)}, u32[]{:S(2)}) collective-permute-start(s32[32,128]{1,0:T(8,128)S(1)} %max.18), channel_id=1, source_target_pairs={{0,16},{1,17},{2,18},{3,19},{4,20},{5,21},{6,22},{7,23},{8,24},{9,... | collective-permute-start | bytes 49160 | tf_op jit(solution)/shard_map/ppermute | solution.py:721
where the time goes:
time: 128 us
  Pallas kernels  56.4 us (44%)
  waiting for transfers between devices  47.4 us (37%)
  starting transfers between devices  21.2 us (17%)
  other arithmetic  2.19 us (2%)
    ppermute x5, waiting for transfers between devices, shifted(): lax.ppermute(value, AXES, [(source, source + steps) for source in range(f...  43.4 us
    pallas_call x1, Pallas kernels, main_part(): call(functools.partial(main_kernel, lists), in_specs=[SMEM, ANY, ANY], ou...  26.4 us
    ppermute x5, starting transfers between devices, shifted(): lax.ppermute(value, AXES, [(source, source + steps) for source in range(f...  15.5 us
    pallas_call x1, Pallas kernels, rest_part(): call(functools.partial(rest_kernel, lists, again), in_specs=[SMEM, ANY, A...  12.2 us
    ppermute x5, starting transfers between devices, merged(): lax.ppermute(value, AXES, [(device, device ^ bit) for device in range(cou...  5.75 us
    pallas_call x1, Pallas kernels, square_diagonals(): call(functools.partial(square_kernel, lists), in_specs=[SMEM, ANY, ANY],...  5.72 us
    pallas_call x1, Pallas kernels, pack_tiles(): call(functools.partial(pack_kernel, lists), in_specs=[SMEM, SMEM, ANY, AN...  4.97 us
    ppermute x5, waiting for transfers between devices, merged(): lax.ppermute(value, AXES, [(device, device ^ bit) for device in range(cou...  4 us
  transfers between devices with their start and end apart: 10, of which 4 were waited for; matrix products, arithmetic and copies ran while one was open for 1% of the time, Pallas kernels for 29%

commit v1 on v0

--- a/solution.py
+++ b/solution.py
@@ -500,15 +500,15 @@
     )(pattern, weights, edges)
 
 
-def list_kernel(lists, back, forward, again, plan, pattern, out, table, index, raw, sums):
+def list_kernel(lists, plan, pattern, out, table, index, raw, sums):
+    back = BACK + MORE[-1][0]
     slots = SLAB * lists
     first_raw = slots + SLAB
     slot_table(table, pattern, 0, lists)
     raw_count = listing(raw, plan, AHEAD, 0)
-    sum_count = jnp.minimum(listing(sums, plan, BEHIND, SLAB), forward)
+    sum_count = listing(sums, plan, BEHIND, SLAB)
     half_count = diagonals_needed(out, DIAGONAL, plan, AHEAD)
     room = lax.shift_right_logical(2 * BACK - half_count, 1)
-    raw_count = jnp.minimum(raw_count, room + (back - BACK))
 
     for row in range(SLAB):
         index[row * BAND] = slots + row
@@ -523,9 +523,8 @@
 
     for place in range(TARGET, PLACE):
         out[place] = 0
-    if not again:
-        for row in range(SLAB):
-            out[TARGET + row * lists] = 1
+    for row in range(SLAB):
+        out[TARGET + row * lists] = 1
 
     def jobs_of(slot, count):
         i = slot // lists
@@ -542,9 +541,6 @@
             ours = table[jnp.clip(column, 0, SLAB - 1) * BAND + gap]
             right = jnp.where(later, theirs, ours)
             valid = (offset >= 0) & (row >= 0) & (left >= 0) & (right >= 0)
-            if again:
-                fresh = first_raw + BACK
-                valid = valid & ((left >= fresh) | (right >= fresh))
             turned = valid & later & ~straight
             out[JOB_SLOT + count] = slot
             out[JOB_LEFT + count] = left
@@ -561,10 +557,7 @@
     def _(k):
         slot = table[sums[k] // BAND * BAND + sums[k] % BAND - sums[k] // BAND]
         out[SUM_SLOT + k] = slot
-        if again:
-            out[TARGET + jnp.where(k >= FORWARD, slot, slots)] = 1
-        else:
-            out[TARGET + slot] = 1
+        out[TARGET + slot] = 1
 
     out[JOBS] = jobs
     out[RAWS] = raw_count
@@ -572,10 +565,10 @@
     out[DIAGONALS] = half_count
 
 
-def product_list(back, forward, again, plan, pattern, lists):
+def product_list(plan, pattern, lists):
     small = pltpu.SMEM((SLAB * BAND,), jnp.int32)
     return call(
-        functools.partial(list_kernel, lists, back, forward, again),
+        functools.partial(list_kernel, lists),
         in_specs=[SMEM, SMEM],
         out_specs=SMEM,
         out_shape=jax.ShapeDtypeStruct((LIST_SIZE,), jnp.int32),
@@ -584,13 +577,13 @@
 
 
 def rest_kernel(
-    lists, again, todo, weights, edges, turned_high, turned_low, squares, message, sums, before, out,
-    w, e, high, low, result, sems, out_sem,
+    lists, todo, weights, edges, turned_high, turned_low, squares, message, sums, more_message, more_sums,
+    before, out, w, e, high, low, result, stage, sems, out_sem, stage_sem,
 ):
     tile = weights.shape[-1]
     half = tile // 2
     slots = SLAB * lists
-    back = message.shape[0] // tile
+    back = (message.shape[0] + more_message.shape[0]) // tile
     first_raw = slots + SLAB
 
     def inputs(slot):
@@ -637,7 +630,19 @@
     @pl.loop(0, todo[RAWS])
     def _(k):
         place = todo[PLACE + k]
-        value = message[pl.ds(pl.multiple_of(place * tile, tile), tile), :]
+
+        @pl.when(place < BACK)
+        def _():
+            stage[...] = message[pl.ds(pl.multiple_of(place * tile, tile), tile), :]
+
+        @pl.when(place >= BACK)
+        def _():
+            rows = pl.ds(pl.multiple_of((place - BACK) * tile, tile), tile)
+            copy = pltpu.make_async_copy(more_message.at[rows], stage, stage_sem)
+            copy.start()
+            copy.wait()
+
+        value = stage[...]
         high[first_raw + place], low[first_raw + place] = split(value)
 
         @pl.when(todo[TURNED + place] == 1)
@@ -657,7 +662,7 @@
                 copy.wait()
             w[slot] = w[slot] * e[slot].astype(F32)
 
-    @pl.loop(0, 0 if again else SLAB)
+    @pl.loop(0, SLAB)
     def _(i):
         def store(first, column, quarter):
             part = (i * lists, pl.ds(first, half), pl.ds(column, half))
@@ -669,10 +674,21 @@
         diagonal = jnp.sum(jnp.where(row == i, rows, 0.0), axis=0, keepdims=True)
         unfold(store, part[:, :half], part[:, half:], diagonal)
 
-    @pl.loop(FORWARD if again else 0, todo[SUMS])
+    @pl.loop(0, todo[SUMS])
     def _(k):
         slot = todo[SUM_SLOT + k]
-        result[slot] += w[slot] * sums[k]
+
+        @pl.when(k < FORWARD)
+        def _():
+            stage[...] = sums[k]
+
+        @pl.when(k >= FORWARD)
+        def _():
+            copy = pltpu.make_async_copy(more_sums.at[k - FORWARD], stage, stage_sem)
+            copy.start()
+            copy.wait()
+
+        result[slot] += w[slot] * stage[...]
 
     @pl.loop(0, todo[JOBS])
     def _(job):
@@ -693,26 +709,28 @@
             output(slot).wait()
 
 
-def rest_part(again, todo, weights, edges, high, low, squares, message, sums, before):
+def rest_part(todo, weights, edges, high, low, squares, message, sums, more_message, more_sums, before):
     _, lists, tile, _ = weights.shape
     slots = SLAB * lists
-    factors = slots + SLAB + 2 * (message.shape[0] // tile)
+    factors = slots + SLAB + 2 * (BACK + MORE[-1][0])
     return call(
-        functools.partial(rest_kernel, lists, again),
-        in_specs=[SMEM, ANY, ANY, ANY, ANY, VMEM, VMEM, VMEM, ANY],
+        functools.partial(rest_kernel, lists),
+        in_specs=[SMEM, ANY, ANY, ANY, ANY, VMEM, VMEM, VMEM, ANY, ANY, ANY],
         out_specs=ANY,
         out_shape=jax.ShapeDtypeStruct(weights.shape, F32),
-        input_output_aliases={8: 0},
+        input_output_aliases={10: 0},
         scratch_shapes=[
             pltpu.VMEM((slots, tile, tile), F32),
             pltpu.VMEM((slots, tile, tile), jnp.int32),
             pltpu.VMEM((factors, tile, tile), BF16),
             pltpu.VMEM((factors, tile, tile), BF16),
             pltpu.VMEM((slots, tile, tile), F32),
+            pltpu.VMEM((tile, tile), F32),
             pltpu.SemaphoreType.DMA((5, slots)),
             pltpu.SemaphoreType.DMA,
+            pltpu.SemaphoreType.DMA,
         ],
-    )(todo, weights, edges, high, low, squares, message, sums, before)
+    )(todo, weights, edges, high, low, squares, message, sums, more_message, more_sums, before)
 
 
 def merged(value, bits):
@@ -747,33 +765,28 @@
     squares_out, pattern = lax.optimization_barrier((squares_out, pattern))
     squares = shifted(squares_out, 1)
 
-    todo = product_list(BACK, FORWARD, False, plan, pattern, lists)
+    todo = product_list(plan, pattern, lists)
     support, high, low = main_part(pattern, weights, edges)
     everyone, support = lax.optimization_barrier((everyone, support))
     _, level = travel_plan(merged(everyone, [bit for bit in bits if bit >= columns]), lists)
-    support = rest_part(
-        False, todo, weights, edges, high, low, squares, message, sums, support
+
+    def branch(back, forward):
+        def run(more_message, more_sums):
+            if not back:
+                return more_message, more_sums
+            tiles = shifted(more_message[: back * tile], -1)
+            partial = shifted(more_sums[:forward], 1)
+            spare = ((0, more_message.shape[0] - back * tile), (0, 0))
+            spare_sums = ((0, more_sums.shape[0] - forward), (0, 0), (0, 0))
+            return jnp.pad(tiles, spare), jnp.pad(partial, spare_sums)
+
+        return run
+
+    more_message, more_sums = lax.switch(
+        level[0], [branch(*sizes) for sizes in MORE], more_message, more_sums
     )
-
-    def branch(back, forward):
-        def run(
-            support, plan, pattern, weights, edges, high, low, squares, message, sums, more_message, more_sums
-        ):
-            if not back:
-                return support
-            message = jnp.concatenate([message, shifted(more_message[: back * tile], -1)])
-            sums = jnp.concatenate([sums, shifted(more_sums[:forward], 1)])
-            todo = product_list(BACK + back, FORWARD + forward, True, plan, pattern, lists)
-            return rest_part(
-                True, todo, weights, edges, high, low, squares, message, sums, support
-            )
-
-        return run
-
-    return lax.switch(
-        level[0],
-        [branch(*sizes) for sizes in MORE],
-        support, plan, pattern, weights, edges, high, low, squares, message, sums, more_message, more_sums,
+    return rest_part(
+        todo, weights, edges, high, low, squares, message, sums, more_message, more_sums, support
     )
 
 

time: 128 us -> 130 us (1.016)
  the two profiles are of different devices: /device:TPU:13 before, /device:TPU:28 now
where the time goes in v1:
time: 130 us; the launch traced here: 128 us
  waiting for transfers between devices  60.4 us (46%)
  Pallas kernels  43.5 us (33%)
  starting transfers between devices  20.1 us (15%)
  other arithmetic  2.18 us (2%)
  local copies, waits for them, and re-layouts  1.44 us (1%)
    ppermute x5, waiting for transfers between devices, shifted(): lax.ppermute(value, AXES, [(source, source + steps) for source in range(f...  53.3 us
    ppermute x5, starting transfers between devices, shifted(): lax.ppermute(value, AXES, [(source, source + steps) for source in range(f...  18.4 us
    pallas_call x1, Pallas kernels, main_part(): call(functools.partial(main_kernel, lists), in_specs=[SMEM, ANY, ANY], ou...  14.1 us
    pallas_call x1, Pallas kernels, rest_part(): call(functools.partial(rest_kernel, lists), in_specs=[SMEM, ANY, ANY, ANY...  10.8 us
    ppermute x5, waiting for transfers between devices, merged(): lax.ppermute(value, AXES, [(device, device ^ bit) for device in range(cou...  7.08 us
    pallas_call x1, Pallas kernels, pack_tiles(): call(functools.partial(pack_kernel, lists), in_specs=[SMEM, SMEM, ANY, AN...  6.21 us
    pallas_call x1, Pallas kernels, square_diagonals(): call(functools.partial(square_kernel, lists), in_specs=[SMEM, ANY, ANY],...  5.1 us
    pallas_call x2, Pallas kernels, travel_plan(): call(functools.partial(plan_kernel, lists), in_specs=[VMEM], out_specs=[V...  3.59 us
  transfers between devices with their start and end apart: 10, of which 6 were waited for; matrix products, arithmetic and copies ran while one was open for 1% of the time, Pallas kernels for 19%

profile of v1, /device:TPU:28, one launch (start us, length us, event | category | flops | bytes accessed | tf_op | source)
XLA Modules:
  0.0 128.4 jit_solution(4644812413129299304)
XLA Ops:
  0.0 0.7 fusion.1
  0.7 0.1 copy.7
  0.8 0.1 reshape.12
  0.9 0.1 broadcast_select_fusion
  1.0 0.5 collective-permute-start.4
  1.5 3.2 %collective-permute-done.4 = s32[32,128]{1,0:T(8,128)S(1)} collective-permute-done((s32[32,128]{1,0:T(8,128)S(1)}, s32[32,128]{1,0:T(8,128)S(1)}, u32[]{:S(2)}, u32[]{:S(2)}) %collective-permute-start.4) | collective-permute-done | bytes 16416 | tf_op jit(solution)/shard_map/ppermute | solution.py:739
  4.7 0.1 fusion
  4.8 0.5 collective-permute-start.5
  5.2 2.4 %collective-permute-start.8 = (s32[1,128]{1,0:T(1,128)S(1)}, s32[1,128]{1,0:T(1,128)S(1)}, u32[]{:S(2)}, u32[]{:S(2)}) collective-permute-start(s32[1,128]{1,0:T(1,128)S(1)} %get-tuple-element.46.pattern), channel_id=1, source_target_pairs={{1,0},{2,1},{3,2},{4,3},{5,4},{6,5},{7,6},{8,7},{9,8},{10,9},{11,1... | collective-permute-start | bytes 1544 | tf_op jit(solution)/shard_map/ppermute | solution.py:32
  7.6 5.8 %collective-permute-start.7 = (s32[1,128]{1,0:T(1,128)S(1)}, s32[1,128]{1,0:T(1,128)S(1)}, u32[]{:S(2)}, u32[]{:S(2)}) collective-permute-start(s32[1,128]{1,0:T(1,128)S(1)} %get-tuple-element.46.pattern), channel_id=1, source_target_pairs={{0,1},{1,2},{2,3},{3,4},{4,5},{5,6},{6,7},{7,8},{8,9},{9,10},{10,1... | collective-permute-start | bytes 1544 | tf_op jit(solution)/shard_map/ppermute | solution.py:32
  13.5 0.1 pad.16.clone
  13.6 0.1 fusion.3
  13.7 1.1 collective-permute-done.7
  14.8 0.7 add_add_fusion.patterns
  15.4 2.9 %collective-permute-done.6 = s32[32,128]{1,0:T(8,128)S(1)} collective-permute-done((s32[32,128]{1,0:T(8,128)S(1)}, s32[32,128]{1,0:T(8,128)S(1)}, u32[]{:S(2)}, u32[]{:S(2)}) %collective-permute-start.6) | collective-permute-done | bytes 16416 | tf_op jit(solution)/shard_map/ppermute | solution.py:739
  18.3 1.6 %shard_map.46 = (s32[8,128]{1,0:T(8,128)}, s32[1]{0:T(128)}) custom-call(s32[8,128]{1,0:T(8,128)} %add_add_fusion.patterns), custom_call_target="tpu_custom_call" | custom-call | tf_op jit(solution)/shard_map/pallas_call | solution.py:237
  19.9 6.2 %shard_map.47 = (f32[2560,256]{1,0:T(8,128)}, f32[3,256,256]{2,1,0:T(8,128)}, f32[2048,256]{1,0:T(8,128)S(1)}, f32[6,256,256]{2,1,0:T(8,128)}) custom-call(s32[8,128]{1,0:T(8,128)} %get-tuple-element.42.plan, s32[1,128]{1,0:T(1,128)} %copy-done.2, f32[5,4,256,256]{3,2,1,0:T(8,128)} %weights.7, s32[5,4,256,256]{3,2,1,0:T(8,128)} %edges.7), custom_call_target="tpu_custom_call" | custom-call | tf_op jit(solution)/shard_map/pallas_call | solution.py:362
  26.2 1.9 %collective-permute-start.10 = (f32[2560,256]{1,0:T(8,128)}, f32[2560,256]{1,0:T(8,128)}, u32[]{:S(2)}, u32[]{:S(2)}) collective-permute-start(f32[2560,256]{1,0:T(8,128)} %get-tuple-element.50), channel_id=1, source_target_pairs={{1,0},{2,1},{3,2},{4,3},{5,4},{6,5},{7,6},{8,7},{9,8},{10,9},{11,1... | collective-permute-start | bytes 7864328 | tf_op jit(solution)/shard_map/ppermute | solution.py:32
  28.1 6.3 %collective-permute-start.11 = (f32[3,256,256]{2,1,0:T(8,128)}, f32[3,256,256]{2,1,0:T(8,128)S(1)}, u32[]{:S(2)}, u32[]{:S(2)}) collective-permute-start(f32[3,256,256]{2,1,0:T(8,128)} %get-tuple-element.51), channel_id=1, source_target_pairs={{0,1},{1,2},{2,3},{3,4},{4,5},{5,6},{6,7},{7,8},{8,9},{9,10},{10,1... | collective-permute-start | bytes 2359304 | tf_op jit(solution)/shard_map/ppermute | solution.py:32
  34.4 5.1 %shard_map.48 = f32[648,256]{1,0:T(8,128)} custom-call(s32[1,128]{1,0:T(1,128)} %copy-done.2, f32[5,4,256,256]{3,2,1,0:T(8,128)} %weights.7, s32[5,4,256,256]{3,2,1,0:T(8,128)} %edges.7), custom_call_target="tpu_custom_call" | custom-call | tf_op jit(solution)/shard_map/pallas_call | solution.py:153
  39.5 1.9 %collective-permute-start.9 = (f32[648,256]{1,0:T(8,128)}, f32[648,256]{1,0:T(8,128)S(1)}, u32[]{:S(2)}, u32[]{:S(2)}) collective-permute-start(f32[648,256]{1,0:T(8,128)} %shard_map.48), channel_id=1, source_target_pairs={{0,1},{1,2},{2,3},{3,4},{4,5},{5,6},{6,7},{7,8},{8,9},{9,10},{10,1... | collective-permute-start | bytes 1990664 | tf_op jit(solution)/shard_map/ppermute | solution.py:32
  41.5 14.1 %shard_map.50 = (f32[5,4,256,256]{3,2,1,0:T(8,128)}, bf16[20,256,256]{2,1,0:T(8,128)(2,1)}, bf16[20,256,256]{2,1,0:T(8,128)(2,1)}) custom-call(s32[1,128]{1,0:T(1,128)} %copy-done.2, f32[5,4,256,256]{3,2,1,0:T(8,128)} %weights.7, s32[5,4,256,256]{3,2,1,0:T(8,128)} %edges.7), custom_call_target="tpu_custom_call" | custom-call | flops 6039797760 | bytes 15728640 | tf_op jit(solution)/shard_map/pallas_call | solution.py:480
  55.6 0.7 collective-permute-start.12
  56.3 0.8 collective-permute-done.12
  57.2 3.6 %shard_map.49.todo = s32[512]{0:T(512)} custom-call(s32[8,128]{1,0:T(8,128)} %get-tuple-element.42.plan, s32[1,128]{1,0:T(1,128)} %copy-done.2), custom_call_target="tpu_custom_call" | custom-call | tf_op jit(solution)/shard_map/pallas_call | solution.py:570
  60.8 0.1 collective-permute-done.13
  60.9 0.6 max.19.patterns
  61.5 2.0 %shard_map.51 = (s32[32,128]{1,0:T(8,128)}, s32[1]{0:T(128)}) custom-call(s32[32,128]{1,0:T(8,128)} %max.19.patterns), custom_call_target="tpu_custom_call" | custom-call | tf_op jit(solution)/shard_map/pallas_call | solution.py:237
  64.1 52.2 %collective-permute-done.9.squares = f32[648,256]{1,0:T(8,128)S(1)} collective-permute-done((f32[648,256]{1,0:T(8,128)}, f32[648,256]{1,0:T(8,128)S(1)}, u32[]{:S(2)}, u32[]{:S(2)}) %collective-permute-start.9) | collective-permute-done | bytes 663584 | tf_op jit(solution)/shard_map/ppermute | solution.py:32
  116.4 0.9 copy-done.1
  117.2 0.3 copy-done
  117.5 10.8 %shard_map.52 = f32[5,4,256,256]{3,2,1,0:T(8,128)} custom-call(s32[512]{0:T(512)} %shard_map.49.todo, f32[5,4,256,256]{3,2,1,0:T(8,128)} %weights.7, s32[5,4,256,256]{3,2,1,0:T(8,128)} %edges.7, bf16[20,256,256]{2,1,0:T(8,128)(2,1)} %get-tuple-element.47.turned_high, ...), custom_call_target="tpu_custom_call", output_to_operand_aliasing={{}: (10, {})} | custom-call | tf_op jit(solution)/shard_map/pallas_call | solution.py:716
  (16 shorter events, 0.1 us)
Async XLA Ops:
  0.9 19.1 %copy-start.2 = (s32[1,128]{1,0:T(1,128)}, s32[1,128]{1,0:T(1,128)S(1)}, u32[]{:S(2)}) copy-start(s32[1,128]{1,0:T(1,128)S(1)} %get-tuple-element.46.pattern) | copy-start | bytes 1540
  1.0 3.7 %collective-permute-start.4 = (s32[32,128]{1,0:T(8,128)S(1)}, s32[32,128]{1,0:T(8,128)S(1)}, u32[]{:S(2)}, u32[]{:S(2)}) collective-permute-start(s32[32,128]{1,0:T(8,128)S(1)} %broadcast_select_fusion), channel_id=1, source_target_pairs={{0,1},{1,0},{2,3},{3,2},{4,5},{5,4},{6,7},{7,6},{8,9},{9,8},{10,11... | collective-permute-start | bytes 49160 | tf_op jit(solution)/shard_map/ppermute | solution.py:739
  4.8 8.8 %collective-permute-start.5 = (s32[32,128]{1,0:T(8,128)S(1)}, s32[32,128]{1,0:T(8,128)S(1)}, u32[]{:S(2)}, u32[]{:S(2)}) collective-permute-start(s32[32,128]{1,0:T(8,128)S(1)} %fusion), channel_id=1, source_target_pairs={{0,2},{1,3},{2,0},{3,1},{4,6},{5,7},{6,4},{7,5},{8,10},{9,11},{10,... | collective-permute-start | bytes 49160 | tf_op jit(solution)/shard_map/ppermute | solution.py:739
  5.2 8.4 %collective-permute-start.8 = (s32[1,128]{1,0:T(1,128)S(1)}, s32[1,128]{1,0:T(1,128)S(1)}, u32[]{:S(2)}, u32[]{:S(2)}) collective-permute-start(s32[1,128]{1,0:T(1,128)S(1)} %get-tuple-element.46.pattern), channel_id=1, source_target_pairs={{1,0},{2,1},{3,2},{4,3},{5,4},{6,5},{7,6},{8,7},{9,8},{10,9},{11,1... | collective-permute-start | bytes 1544 | tf_op jit(solution)/shard_map/ppermute | solution.py:32
  7.6 7.1 %collective-permute-start.7 = (s32[1,128]{1,0:T(1,128)S(1)}, s32[1,128]{1,0:T(1,128)S(1)}, u32[]{:S(2)}, u32[]{:S(2)}) collective-permute-start(s32[1,128]{1,0:T(1,128)S(1)} %get-tuple-element.46.pattern), channel_id=1, source_target_pairs={{0,1},{1,2},{2,3},{3,4},{4,5},{5,6},{6,7},{7,8},{8,9},{9,10},{10,1... | collective-permute-start | bytes 1544 | tf_op jit(solution)/shard_map/ppermute | solution.py:32
  13.7 4.6 %collective-permute-start.6 = (s32[32,128]{1,0:T(8,128)S(1)}, s32[32,128]{1,0:T(8,128)S(1)}, u32[]{:S(2)}, u32[]{:S(2)}) collective-permute-start(s32[32,128]{1,0:T(8,128)S(1)} %fusion.3), channel_id=1, source_target_pairs={{0,4},{1,5},{2,6},{3,7},{4,0},{5,1},{6,2},{7,3},{8,12},{9,13},{10,... | collective-permute-start | bytes 49160 | tf_op jit(solution)/shard_map/ppermute | solution.py:739
  26.2 90.2 %collective-permute-start.10 = (f32[2560,256]{1,0:T(8,128)}, f32[2560,256]{1,0:T(8,128)}, u32[]{:S(2)}, u32[]{:S(2)}) collective-permute-start(f32[2560,256]{1,0:T(8,128)} %get-tuple-element.50), channel_id=1, source_target_pairs={{1,0},{2,1},{3,2},{4,3},{5,4},{6,5},{7,6},{8,7},{9,8},{10,9},{11,1... | collective-permute-start | bytes 7864328 | tf_op jit(solution)/shard_map/ppermute | solution.py:32
  28.1 88.3 %collective-permute-start.11 = (f32[3,256,256]{2,1,0:T(8,128)}, f32[3,256,256]{2,1,0:T(8,128)S(1)}, u32[]{:S(2)}, u32[]{:S(2)}) collective-permute-start(f32[3,256,256]{2,1,0:T(8,128)} %get-tuple-element.51), channel_id=1, source_target_pairs={{0,1},{1,2},{2,3},{3,4},{4,5},{5,6},{6,7},{7,8},{8,9},{9,10},{10,1... | collective-permute-start | bytes 2359304 | tf_op jit(solution)/shard_map/ppermute | solution.py:32
  39.5 76.8 %collective-permute-start.9 = (f32[648,256]{1,0:T(8,128)}, f32[648,256]{1,0:T(8,128)S(1)}, u32[]{:S(2)}, u32[]{:S(2)}) collective-permute-start(f32[648,256]{1,0:T(8,128)} %shard_map.48), channel_id=1, source_target_pairs={{0,1},{1,2},{2,3},{3,4},{4,5},{5,6},{6,7},{7,8},{8,9},{9,10},{10,1... | collective-permute-start | bytes 1990664 | tf_op jit(solution)/shard_map/ppermute | solution.py:32
  55.6 1.6 %collective-permute-start.12 = (s32[32,128]{1,0:T(8,128)S(1)}, s32[32,128]{1,0:T(8,128)S(1)}, u32[]{:S(2)}, u32[]{:S(2)}) collective-permute-start(s32[32,128]{1,0:T(8,128)S(1)} %max.17), channel_id=1, source_target_pairs={{0,8},{1,9},{2,10},{3,11},{4,12},{5,13},{6,14},{7,15},{8,0},{9,1},... | collective-permute-start | bytes 49160 | tf_op jit(solution)/shard_map/ppermute | solution.py:739
  57.2 3.7 %collective-permute-start.13 = (s32[32,128]{1,0:T(8,128)S(1)}, s32[32,128]{1,0:T(8,128)S(1)}, u32[]{:S(2)}, u32[]{:S(2)}) collective-permute-start(s32[32,128]{1,0:T(8,128)S(1)} %max.18), channel_id=1, source_target_pairs={{0,16},{1,17},{2,18},{3,19},{4,20},{5,21},{6,22},{7,23},{8,24},{9,... | collective-permute-start | bytes 49160 | tf_op jit(solution)/shard_map/ppermute | solution.py:739
  116.3 0.9 copy-start.1
  116.3 1.2 copy-start

commit v2 on v1

--- a/solution.py
+++ b/solution.py
@@ -12,7 +12,7 @@
 LANES = 128
 AXES = ("row", "col")
 BACK, FORWARD = 10, 3
-MORE = ((0, 0), (2, 1), (8, 6))
+MORE = ((0, 0), (1, 1), (2, 1), (3, 2), (8, 6))
 BEHIND, AHEAD = 0, 1
 JOBS, RAWS, SUMS, DIAGONALS = 0, 1, 2, 3
 TARGET, FACTOR, TURNED, PLACE, SUM_SLOT, DIAGONAL = 8, 32, 64, 96, 128, 144

time: 130 us -> 130 us (level)
  the two profiles are of different devices: /device:TPU:28 before, /device:TPU:13 now
where the time goes in v2:
time: 130 us; the launch traced here: 129 us
  waiting for transfers between devices  51.2 us (39%)
  Pallas kernels  48.3 us (37%)
  starting transfers between devices  24.9 us (19%)
  other arithmetic  2.19 us (2%)
  local copies, waits for them, and re-layouts  1.43 us (1%)
    ppermute x5, waiting for transfers between devices, shifted(): lax.ppermute(value, AXES, [(source, source + steps) for source in range(f...  47.5 us
    pallas_call x1, Pallas kernels, main_part(): call(functools.partial(main_kernel, lists), in_specs=[SMEM, ANY, ANY], ou...  19.4 us
    ppermute x5, starting transfers between devices, shifted(): lax.ppermute(value, AXES, [(source, source + steps) for source in range(f...  14.3 us
    pallas_call x1, Pallas kernels, rest_part(): call(functools.partial(rest_kernel, lists), in_specs=[SMEM, ANY, ANY, ANY...  11 us
    ppermute x5, starting transfers between devices, merged(): lax.ppermute(value, AXES, [(device, device ^ bit) for device in range(cou...  10.6 us
    pallas_call x1, Pallas kernels, pack_tiles(): call(functools.partial(pack_kernel, lists), in_specs=[SMEM, SMEM, ANY, AN...  5.49 us
    pallas_call x1, Pallas kernels, square_diagonals(): call(functools.partial(square_kernel, lists), in_specs=[SMEM, ANY, ANY],...  5.26 us
    ppermute x5, waiting for transfers between devices, merged(): lax.ppermute(value, AXES, [(device, device ^ bit) for device in range(cou...  3.67 us
  transfers between devices with their start and end apart: 10, of which 4 were waited for; matrix products, arithmetic and copies ran while one was open for 1% of the time, Pallas kernels for 23%

profile of v2, /device:TPU:13, one launch (start us, length us, event | category | flops | bytes accessed | tf_op | source)
XLA Modules:
  0.0 128.7 jit_solution(17617267540146876956)
XLA Ops:
  0.0 0.7 fusion.1
  0.7 0.1 copy.7
  0.8 0.1 reshape.12
  0.9 0.1 broadcast_select_fusion
  1.0 0.2 collective-permute-start.8
  1.2 2.4 %collective-permute-done.8 = s32[32,128]{1,0:T(8,128)S(1)} collective-permute-done((s32[32,128]{1,0:T(8,128)S(1)}, s32[32,128]{1,0:T(8,128)S(1)}, u32[]{:S(2)}, u32[]{:S(2)}) %collective-permute-start.8) | collective-permute-done | bytes 16416 | tf_op jit(solution)/shard_map/ppermute | solution.py:739
  3.5 0.1 fusion
  3.6 0.2 collective-permute-start.9
  3.8 2.0 %collective-permute-start.12 = (s32[1,128]{1,0:T(1,128)S(1)}, s32[1,128]{1,0:T(1,128)S(1)}, u32[]{:S(2)}, u32[]{:S(2)}) collective-permute-start(s32[1,128]{1,0:T(1,128)S(1)} %get-tuple-element.58.pattern), channel_id=1, source_target_pairs={{1,0},{2,1},{3,2},{4,3},{5,4},{6,5},{7,6},{8,7},{9,8},{10,9},{11,1... | collective-permute-start | bytes 1544 | tf_op jit(solution)/shard_map/ppermute | solution.py:32
  5.8 4.2 %collective-permute-start.11 = (s32[1,128]{1,0:T(1,128)S(1)}, s32[1,128]{1,0:T(1,128)S(1)}, u32[]{:S(2)}, u32[]{:S(2)}) collective-permute-start(s32[1,128]{1,0:T(1,128)S(1)} %get-tuple-element.58.pattern), channel_id=1, source_target_pairs={{0,1},{1,2},{2,3},{3,4},{4,5},{5,6},{6,7},{7,8},{8,9},{9,10},{10,1... | collective-permute-start | bytes 1544 | tf_op jit(solution)/shard_map/ppermute | solution.py:32
  10.0 0.1 pad.31.clone
  10.1 0.1 fusion.3
  10.2 5.3 %collective-permute-start.10 = (s32[32,128]{1,0:T(8,128)S(1)}, s32[32,128]{1,0:T(8,128)S(1)}, u32[]{:S(2)}, u32[]{:S(2)}) collective-permute-start(s32[32,128]{1,0:T(8,128)S(1)} %fusion.3), channel_id=1, source_target_pairs={{0,4},{1,5},{2,6},{3,7},{4,0},{5,1},{6,2},{7,3},{8,12},{9,13},{10,... | collective-permute-start | bytes 49160 | tf_op jit(solution)/shard_map/ppermute | solution.py:739
  15.4 0.0 collective-permute-done.12
  15.4 0.7 add_add_fusion.patterns
  16.1 0.5 collective-permute-done.10
  16.6 1.6 %shard_map.46 = (s32[8,128]{1,0:T(8,128)}, s32[1]{0:T(128)}) custom-call(s32[8,128]{1,0:T(8,128)} %add_add_fusion.patterns), custom_call_target="tpu_custom_call" | custom-call | tf_op jit(solution)/shard_map/pallas_call | solution.py:237
  18.2 5.5 %shard_map.47 = (f32[2560,256]{1,0:T(8,128)}, f32[3,256,256]{2,1,0:T(8,128)}, f32[2048,256]{1,0:T(8,128)S(1)}, f32[6,256,256]{2,1,0:T(8,128)}) custom-call(s32[8,128]{1,0:T(8,128)} %get-tuple-element.54.plan, s32[1,128]{1,0:T(1,128)} %copy-done.2, f32[5,4,256,256]{3,2,1,0:T(8,128)} %weights.7, s32[5,4,256,256]{3,2,1,0:T(8,128)} %edges.7), custom_call_target="tpu_custom_call" | custom-call | tf_op jit(solution)/shard_map/pallas_call | solution.py:362
  23.7 1.9 %collective-permute-start.14 = (f32[2560,256]{1,0:T(8,128)}, f32[2560,256]{1,0:T(8,128)}, u32[]{:S(2)}, u32[]{:S(2)}) collective-permute-start(f32[2560,256]{1,0:T(8,128)} %get-tuple-element.62), channel_id=1, source_target_pairs={{1,0},{2,1},{3,2},{4,3},{5,4},{6,5},{7,6},{8,7},{9,8},{10,9},{11,1... | collective-permute-start | bytes 7864328 | tf_op jit(solution)/shard_map/ppermute | solution.py:32
  25.6 4.3 %collective-permute-start.15 = (f32[3,256,256]{2,1,0:T(8,128)}, f32[3,256,256]{2,1,0:T(8,128)S(1)}, u32[]{:S(2)}, u32[]{:S(2)}) collective-permute-start(f32[3,256,256]{2,1,0:T(8,128)} %get-tuple-element.63), channel_id=1, source_target_pairs={{0,1},{1,2},{2,3},{3,4},{4,5},{5,6},{6,7},{7,8},{8,9},{9,10},{10,1... | collective-permute-start | bytes 2359304 | tf_op jit(solution)/shard_map/ppermute | solution.py:32
  29.9 5.3 %shard_map.48 = f32[648,256]{1,0:T(8,128)} custom-call(s32[1,128]{1,0:T(1,128)} %copy-done.2, f32[5,4,256,256]{3,2,1,0:T(8,128)} %weights.7, s32[5,4,256,256]{3,2,1,0:T(8,128)} %edges.7), custom_call_target="tpu_custom_call" | custom-call | tf_op jit(solution)/shard_map/pallas_call | solution.py:153
  35.2 1.9 %collective-permute-start.13 = (f32[648,256]{1,0:T(8,128)}, f32[648,256]{1,0:T(8,128)S(1)}, u32[]{:S(2)}, u32[]{:S(2)}) collective-permute-start(f32[648,256]{1,0:T(8,128)} %shard_map.48), channel_id=1, source_target_pairs={{0,1},{1,2},{2,3},{3,4},{4,5},{5,6},{6,7},{7,8},{8,9},{9,10},{10,1... | collective-permute-start | bytes 1990664 | tf_op jit(solution)/shard_map/ppermute | solution.py:32
  37.1 19.4 %shard_map.50 = (f32[5,4,256,256]{3,2,1,0:T(8,128)}, bf16[20,256,256]{2,1,0:T(8,128)(2,1)}, bf16[20,256,256]{2,1,0:T(8,128)(2,1)}) custom-call(s32[1,128]{1,0:T(1,128)} %copy-done.2, f32[5,4,256,256]{3,2,1,0:T(8,128)} %weights.7, s32[5,4,256,256]{3,2,1,0:T(8,128)} %edges.7), custom_call_target="tpu_custom_call" | custom-call | flops 6039797760 | bytes 15728640 | tf_op jit(solution)/shard_map/pallas_call | solution.py:480
  56.5 4.9 %collective-permute-start.16 = (s32[32,128]{1,0:T(8,128)S(1)}, s32[32,128]{1,0:T(8,128)S(1)}, u32[]{:S(2)}, u32[]{:S(2)}) collective-permute-start(s32[32,128]{1,0:T(8,128)S(1)} %max.17), channel_id=1, source_target_pairs={{0,8},{1,9},{2,10},{3,11},{4,12},{5,13},{6,14},{7,15},{8,0},{9,1},... | collective-permute-start | bytes 49160 | tf_op jit(solution)/shard_map/ppermute | solution.py:739
  61.4 0.8 collective-permute-done.16
  62.2 3.6 %shard_map.49.todo = s32[512]{0:T(512)} custom-call(s32[8,128]{1,0:T(8,128)} %get-tuple-element.54.plan, s32[1,128]{1,0:T(1,128)} %copy-done.2), custom_call_target="tpu_custom_call" | custom-call | tf_op jit(solution)/shard_map/pallas_call | solution.py:570
  65.8 0.6 max.19.patterns
  66.4 2.0 %shard_map.51 = (s32[32,128]{1,0:T(8,128)}, s32[1]{0:T(128)}) custom-call(s32[32,128]{1,0:T(8,128)} %max.19.patterns), custom_call_target="tpu_custom_call" | custom-call | tf_op jit(solution)/shard_map/pallas_call | solution.py:237
  69.1 47.5 %collective-permute-done.13.squares = f32[648,256]{1,0:T(8,128)S(1)} collective-permute-done((f32[648,256]{1,0:T(8,128)}, f32[648,256]{1,0:T(8,128)S(1)}, u32[]{:S(2)}, u32[]{:S(2)}) %collective-permute-start.13) | collective-permute-done | bytes 663584 | tf_op jit(solution)/shard_map/ppermute | solution.py:32
  116.6 0.9 copy-done.1
  117.4 0.3 copy-done
  117.7 11.0 %shard_map.52 = f32[5,4,256,256]{3,2,1,0:T(8,128)} custom-call(s32[512]{0:T(512)} %shard_map.49.todo, f32[5,4,256,256]{3,2,1,0:T(8,128)} %weights.7, s32[5,4,256,256]{3,2,1,0:T(8,128)} %edges.7, bf16[20,256,256]{2,1,0:T(8,128)(2,1)} %get-tuple-element.59.turned_high, ...), custom_call_target="tpu_custom_call", output_to_operand_aliasing={{}: (10, {})} | custom-call | tf_op jit(solution)/shard_map/pallas_call | solution.py:716
  (16 shorter events, 0.1 us)
Async XLA Ops:
  0.9 17.3 %copy-start.2 = (s32[1,128]{1,0:T(1,128)}, s32[1,128]{1,0:T(1,128)S(1)}, u32[]{:S(2)}) copy-start(s32[1,128]{1,0:T(1,128)S(1)} %get-tuple-element.58.pattern) | copy-start | bytes 1540
  1.0 2.6 %collective-permute-start.8 = (s32[32,128]{1,0:T(8,128)S(1)}, s32[32,128]{1,0:T(8,128)S(1)}, u32[]{:S(2)}, u32[]{:S(2)}) collective-permute-start(s32[32,128]{1,0:T(8,128)S(1)} %broadcast_select_fusion), channel_id=1, source_target_pairs={{0,1},{1,0},{2,3},{3,2},{4,5},{5,4},{6,7},{7,6},{8,9},{9,8},{10,11... | collective-permute-start | bytes 49160 | tf_op jit(solution)/shard_map/ppermute | solution.py:739
  3.6 6.5 %collective-permute-start.9 = (s32[32,128]{1,0:T(8,128)S(1)}, s32[32,128]{1,0:T(8,128)S(1)}, u32[]{:S(2)}, u32[]{:S(2)}) collective-permute-start(s32[32,128]{1,0:T(8,128)S(1)} %fusion), channel_id=1, source_target_pairs={{0,2},{1,3},{2,0},{3,1},{4,6},{5,7},{6,4},{7,5},{8,10},{9,11},{10,... | collective-permute-start | bytes 49160 | tf_op jit(solution)/shard_map/ppermute | solution.py:739
  3.8 11.6 %collective-permute-start.12 = (s32[1,128]{1,0:T(1,128)S(1)}, s32[1,128]{1,0:T(1,128)S(1)}, u32[]{:S(2)}, u32[]{:S(2)}) collective-permute-start(s32[1,128]{1,0:T(1,128)S(1)} %get-tuple-element.58.pattern), channel_id=1, source_target_pairs={{1,0},{2,1},{3,2},{4,3},{5,4},{6,5},{7,6},{8,7},{9,8},{10,9},{11,1... | collective-permute-start | bytes 1544 | tf_op jit(solution)/shard_map/ppermute | solution.py:32
  5.8 9.7 %collective-permute-start.11 = (s32[1,128]{1,0:T(1,128)S(1)}, s32[1,128]{1,0:T(1,128)S(1)}, u32[]{:S(2)}, u32[]{:S(2)}) collective-permute-start(s32[1,128]{1,0:T(1,128)S(1)} %get-tuple-element.58.pattern), channel_id=1, source_target_pairs={{0,1},{1,2},{2,3},{3,4},{4,5},{5,6},{6,7},{7,8},{8,9},{9,10},{10,1... | collective-permute-start | bytes 1544 | tf_op jit(solution)/shard_map/ppermute | solution.py:32
  10.2 6.4 %collective-permute-start.10 = (s32[32,128]{1,0:T(8,128)S(1)}, s32[32,128]{1,0:T(8,128)S(1)}, u32[]{:S(2)}, u32[]{:S(2)}) collective-permute-start(s32[32,128]{1,0:T(8,128)S(1)} %fusion.3), channel_id=1, source_target_pairs={{0,4},{1,5},{2,6},{3,7},{4,0},{5,1},{6,2},{7,3},{8,12},{9,13},{10,... | collective-permute-start | bytes 49160 | tf_op jit(solution)/shard_map/ppermute | solution.py:739
  23.7 92.9 %collective-permute-start.14 = (f32[2560,256]{1,0:T(8,128)}, f32[2560,256]{1,0:T(8,128)}, u32[]{:S(2)}, u32[]{:S(2)}) collective-permute-start(f32[2560,256]{1,0:T(8,128)} %get-tuple-element.62), channel_id=1, source_target_pairs={{1,0},{2,1},{3,2},{4,3},{5,4},{6,5},{7,6},{8,7},{9,8},{10,9},{11,1... | collective-permute-start | bytes 7864328 | tf_op jit(solution)/shard_map/ppermute | solution.py:32
  25.6 90.9 %collective-permute-start.15 = (f32[3,256,256]{2,1,0:T(8,128)}, f32[3,256,256]{2,1,0:T(8,128)S(1)}, u32[]{:S(2)}, u32[]{:S(2)}) collective-permute-start(f32[3,256,256]{2,1,0:T(8,128)} %get-tuple-element.63), channel_id=1, source_target_pairs={{0,1},{1,2},{2,3},{3,4},{4,5},{5,6},{6,7},{7,8},{8,9},{9,10},{10,1... | collective-permute-start | bytes 2359304 | tf_op jit(solution)/shard_map/ppermute | solution.py:32
  35.2 81.4 %collective-permute-start.13 = (f32[648,256]{1,0:T(8,128)}, f32[648,256]{1,0:T(8,128)S(1)}, u32[]{:S(2)}, u32[]{:S(2)}) collective-permute-start(f32[648,256]{1,0:T(8,128)} %shard_map.48), channel_id=1, source_target_pairs={{0,1},{1,2},{2,3},{3,4},{4,5},{5,6},{6,7},{7,8},{8,9},{9,10},{10,1... | collective-permute-start | bytes 1990664 | tf_op jit(solution)/shard_map/ppermute | solution.py:32
  56.5 5.7 %collective-permute-start.16 = (s32[32,128]{1,0:T(8,128)S(1)}, s32[32,128]{1,0:T(8,128)S(1)}, u32[]{:S(2)}, u32[]{:S(2)}) collective-permute-start(s32[32,128]{1,0:T(8,128)S(1)} %max.17), channel_id=1, source_target_pairs={{0,8},{1,9},{2,10},{3,11},{4,12},{5,13},{6,14},{7,15},{8,0},{9,1},... | collective-permute-start | bytes 49160 | tf_op jit(solution)/shard_map/ppermute | solution.py:739
  62.2 3.6 %collective-permute-start.17 = (s32[32,128]{1,0:T(8,128)S(1)}, s32[32,128]{1,0:T(8,128)S(1)}, u32[]{:S(2)}, u32[]{:S(2)}) collective-permute-start(s32[32,128]{1,0:T(8,128)S(1)} %max.18), channel_id=1, source_target_pairs={{0,16},{1,17},{2,18},{3,19},{4,20},{5,21},{6,22},{7,23},{8,24},{9,... | collective-permute-start | bytes 49160 | tf_op jit(solution)/shard_map/ppermute | solution.py:739
  116.6 0.9 copy-start.1
  116.6 1.2 copy-start
